TPU v7x, 512 devices: a whole 4x4x16 slice. The times are simulated.
512 devices in a mesh: dp: 8 (over x, core), expert: 64 (over z, y).
Axes of the slice: x: 4, y: 4, z: 16, core: 2. Of those that a mesh axis runs over, the one named last changes fastest.
Arguments:
- tokens: bfloat16 [16384, 4096], P('expert', 'dp'), may hold values from -6 to 6
- chosen: int32 [64, 64, 4], P('expert'), may hold values from 0 to 255, as said below
- counts: int32 [64, 64], P('expert'), may hold values from 0 to 4, as said below
- gates: float32 [64, 64, 4], P('expert'), may hold values from 0.25 to 1.5
- expert_gate: bfloat16 [64, 4096, 1024], P('expert', None, 'dp'), may hold values from -0.09375 to 0.09375
- expert_up: bfloat16 [64, 4096, 1024], P('expert', None, 'dp'), may hold values from -0.09375 to 0.09375
- expert_down: bfloat16 [64, 1024, 4096], P('expert', 'dp'), may hold values from -0.1875 to 0.1875
- shared_gate: bfloat16 [4096, 2048], P('expert', 'dp'), may hold values from -0.09375 to 0.09375
- shared_up: bfloat16 [4096, 2048], P('expert', 'dp'), may hold values from -0.09375 to 0.09375
- shared_down: bfloat16 [2048, 4096], P('dp', 'expert'), may hold values from -0.125 to 0.125
Outputs:
- mixed: bfloat16 [16384, 4096], P('expert', 'dp')
Inputs may be any that keep to these rules, and one draw needn't show every extreme that they name: chosen[e, j, s] is a row among the 256 tokens of index j of expert; for each e and j the 4 rows are distinct; only the first counts[e, j] slots are live. `counts`: some expert has all 4 slots live for every index of expert.
All inputs are finite; a program needn't handle non-finite values.
Results may differ from a plain program's by a relative error of at most 0.019.
Values may be sent and summed in bfloat16 or wider, within the bound.
A program may use at most 64 MiB of HBM per device.

v0:
```python
import jax
import jax.numpy as jnp
from jax import lax
from jax.sharding import PartitionSpec as P


def shards(
    tokens,
    chosen,
    counts,
    gates,
    expert_gate,
    expert_up,
    expert_down,
    shared_gate,
    shared_up,
    shared_down,
):
    gathered = lax.all_gather(tokens, "dp", axis=1, tiled=True)
    row_count = gathered.shape[0]
    full_width = gathered.shape[1]
    s_gate = jnp.dot(
        gathered,
        lax.all_gather(shared_gate, "expert", axis=0, tiled=True),
        preferred_element_type=jnp.float32,
    )
    s_up = jnp.dot(
        gathered,
        lax.all_gather(shared_up, "expert", axis=0, tiled=True),
        preferred_element_type=jnp.float32,
    )
    shared_hidden = (jax.nn.silu(s_gate) * s_up).astype(jnp.bfloat16)
    shared_terms = jnp.dot(
        shared_hidden,
        lax.all_gather(shared_down, "expert", axis=1, tiled=True),
        preferred_element_type=jnp.float32,
    )
    shared_part = lax.psum_scatter(
        shared_terms.astype(jnp.bfloat16), "dp", scatter_dimension=1, tiled=True
    ).astype(jnp.float32)
    owner_count = chosen.shape[1]
    slot_count = chosen.shape[2]
    picked = lax.all_to_all(chosen, "expert", split_axis=1, concat_axis=0, tiled=True).reshape(
        owner_count * slot_count
    )
    outgoing = jnp.take(tokens, picked, axis=0).reshape(owner_count, slot_count, tokens.shape[1])
    slice_part = lax.all_to_all(outgoing, "expert", split_axis=0, concat_axis=0, tiled=True)
    arrived = lax.all_gather(slice_part, "dp", axis=2, tiled=True)
    flattened = arrived.reshape(owner_count * slot_count, full_width)
    e_gate = jnp.dot(flattened, expert_gate[0], preferred_element_type=jnp.float32)
    e_up = jnp.dot(flattened, expert_up[0], preferred_element_type=jnp.float32)
    e_hidden = (jax.nn.silu(e_gate) * e_up).astype(jnp.bfloat16)
    e_terms = jnp.dot(e_hidden, expert_down[0], preferred_element_type=jnp.float32).reshape(
        owner_count, slot_count, full_width
    )
    e_summed = lax.psum_scatter(
        e_terms.astype(jnp.bfloat16), "dp", scatter_dimension=2, tiled=True
    ).astype(jnp.float32)
    live_mask = lax.broadcasted_iota(jnp.int32, (owner_count, slot_count), 1) < counts[0][:, None]
    slot_weight = jnp.where(live_mask, gates[0], jnp.zeros_like(gates[0]))
    weighted = (e_summed * slot_weight[:, :, None]).astype(jnp.bfloat16)
    returned = lax.all_to_all(weighted, "expert", split_axis=0, concat_axis=0, tiled=True)
    one_hot = (
        picked[None, :] == lax.broadcasted_iota(jnp.int32, (row_count, owner_count * slot_count), 0)
    ).astype(jnp.bfloat16)
    routed = jnp.dot(
        one_hot,
        returned.reshape(owner_count * slot_count, returned.shape[2]),
        preferred_element_type=jnp.float32,
    )
    return (shared_part + routed).astype(jnp.bfloat16)


def solution(mesh):
    return jax.shard_map(
        shards,
        mesh=mesh,
        in_specs=(
            P("expert", "dp"),
            P("expert", None, None),
            P("expert", None),
            P("expert", None, None),
            P("expert", None, "dp"),
            P("expert", None, "dp"),
            P("expert", "dp", None),
            P("expert", "dp"),
            P("expert", "dp"),
            P("dp", "expert"),
        ),
        out_specs=P("expert", "dp"),
        check_vma=False,
    )
```

profile of v0, /device:TPU:1, one launch (start us, length us, event | category | flops | bytes accessed | tf_op | source)
XLA Modules:
  0.0 646.0 jit_solution(2429578908863697231)
XLA Ops:
  6.5 0.9 copy.18
  7.4 32.5 %all_to_all.19 = s32[1,64,4]{2,0,1:T(1,128)S(1)} all-to-all(s32[1,64,4]{2,0,1:T(1,128)S(1)} %copy.18), channel_id=1, replica_groups=mesh['dp'=8,'expert'=64] {'expert'}, dimensions={1} | all-to-all | bytes 2048 | tf_op jit(solution)/shard_map/all_to_all | solution.py:43
  39.9 0.1 reshape.86
  40.1 2.2 gather_fusion
  42.3 0.2 broadcast_select_fusion
  42.6 22.9 %all_to_all.20 = bf16[64,4,512]{2,1,0:T(4,128)(2,1)} all-to-all(bf16[64,4,512]{2,1,0:T(4,128)(2,1)S(1)} %broadcast_select_fusion), channel_id=1, replica_groups=mesh['dp'=8,'expert'=64] {'expert'}, dimensions={0} | all-to-all | bytes 524288 | tf_op jit(solution)/shard_map/all_to_all | solution.py:47
  65.5 0.7 all-gather.6.cloned.1.call-update
  66.2 0.7 all-gather.8.cloned.1.call-update
  67.0 0.5 all-gather.10.cloned.1.call-update
  67.5 0.5 all-gather.12.cloned.1.call-update
  68.1 27.9 %all-gather.14.cloned.1.call-done = bf16[64,4,4096]{2,1,0:T(4,128)(2,1)} async-done(((bf16[64,4,512]{2,1,0:T(4,128)(2,1)}), bf16[64,4,4096]{2,1,0:T(4,128)(2,1)}) %all-gather.14.cloned.1.call-update) | async-done | bytes 2097168 | tf_op jit(solution)/shard_map/all_gather | solution.py:48
  96.0 2.5 reshape.87
  98.5 2.0 fusion.5
  100.6 0.7 fusion.2
  101.3 2.1 convolution_convert_fusion
  103.4 28.6 %all-gather.6.cloned.1.call-done = bf16[256,4096]{1,0:T(8,128)(2,1)} async-done(((bf16[256,512]{1,0:T(8,128)(2,1)}), bf16[256,4096]{1,0:T(8,128)(2,1)}) %all-gather.6.cloned.1.call-update) | async-done | bytes 2097168 | tf_op jit(solution)/shard_map/all_gather | solution.py:19
  132.0 135.1 %all-gather.8.cloned.1.call-done = bf16[4096,256]{1,0:T(8,128)(2,1)} async-done(((bf16[64,256]{1,0:T(8,128)(2,1)}), bf16[4096,256]{1,0:T(8,128)(2,1)}) %all-gather.8.cloned.1.call-update) | async-done | bytes 2097168 | tf_op jit(solution)/shard_map/all_gather | solution.py:24
  267.1 2.9 fusion.16
  270.1 136.9 %all-gather.10.cloned.1.call-done = bf16[4096,256]{1,0:T(8,128)(2,1)} async-done(((bf16[64,256]{1,0:T(8,128)(2,1)}), bf16[4096,256]{1,0:T(8,128)(2,1)}) %all-gather.10.cloned.1.call-update) | async-done | bytes 2097168 | tf_op jit(solution)/shard_map/all_gather | solution.py:29
  406.9 139.8 %all-gather.12.cloned.1.call-done = bf16[256,4096]{0,1:T(8,128)(2,1)} async-done(((bf16[256,64]{0,1:T(8,128)(2,1)}), bf16[256,4096]{0,1:T(8,128)(2,1)}) %all-gather.12.cloned.1.call-update) | async-done | bytes 2097168 | tf_op jit(solution)/shard_map/all_gather | solution.py:35
  546.7 5.9 convolution_convert_fusion.1
  552.7 0.7 copy-done.2
  553.3 40.4 %reduce-scatter.5.cloned.1.call-done = bf16[64,4,512]{2,0,1:T(8,128)(2,1)} async-done(((bf16[64,4,4096]{2,0,1:T(8,128)(2,1)}), bf16[64,4,512]{2,0,1:T(8,128)(2,1)}) %reduce-scatter.5.cloned.1.call-update) | async-done | bytes 262160 | tf_op jit(solution)/shard_map/reduce_scatter | solution.py:56
  593.7 1.1 multiply_convert_fusion
  594.8 0.9 copy.20
  595.7 14.3 %all-to-all-start.2 = ((bf16[64,4,512]{2,1,0:T(4,128)(2,1)}), bf16[64,4,512]{2,1,0:T(4,128)(2,1)S(1)}, u32[]{:S(2)}, u32[]{:S(2)}) async-start(bf16[64,4,512]{2,1,0:T(4,128)(2,1)} %copy.20), calls=%async_computation.4 | async-start | bytes 524288 | tf_op jit(solution)/shard_map/all_to_all | solution.py:62
  610.0 0.6 broadcast.59
  610.6 0.8 reduce.5
  611.4 0.1 eq.12
  611.5 16.1 %all-to-all-done.2 = bf16[64,4,512]{2,1,0:T(4,128)(2,1)S(1)} async-done(((bf16[64,4,512]{2,1,0:T(4,128)(2,1)}), bf16[64,4,512]{2,1,0:T(4,128)(2,1)S(1)}, u32[]{:S(2)}, u32[]{:S(2)}) %all-to-all-start.2) | async-done | bytes 262176 | tf_op jit(solution)/shard_map/all_to_all | solution.py:62
  627.6 9.6 %reduce-scatter.3.cloned.1.call-done = bf16[256,512]{1,0:T(8,128)(2,1)} async-done(((bf16[256,4096]{1,0:T(8,128)(2,1)}), bf16[256,512]{1,0:T(8,128)(2,1)}) %reduce-scatter.3.cloned.1.call-update) | async-done | bytes 262160 | tf_op jit(solution)/shard_map/reduce_scatter | solution.py:38
  637.2 1.9 fusion
  (25 shorter events, 0.5 us)
Async XLA Ops:
  6.5 94.7 %copy-start = (bf16[1,128,4096]{2,1,0:T(8,128)(2,1)S(1)}, bf16[1,128,4096]{2,1,0:T(8,128)(2,1)}, u32[]{:S(2)}) copy-start(bf16[1,128,4096]{2,1,0:T(8,128)(2,1)} %param.16) | copy-start | bytes 3145732
  6.5 89.4 %all-gather.14.cloned.1.call-start = ((), (), s32[]{:S(2)}) async-start(), calls=%async_computation.10 | async-start | bytes 2359296 | tf_op jit(solution)/shard_map/all_gather | solution.py:48
  65.4 66.6 %all-gather.6.cloned.1.call-start = ((), (), s32[]{:S(2)}) async-start(), calls=%async_computation.5 | async-start | bytes 2359296 | tf_op jit(solution)/shard_map/all_gather | solution.py:19
  66.2 200.9 %all-gather.8.cloned.1.call-start = ((), (), s32[]{:S(2)}) async-start(), calls=%async_computation.6 | async-start | bytes 2129920 | tf_op jit(solution)/shard_map/all_gather | solution.py:24
  66.9 340.0 %all-gather.10.cloned.1.call-start = ((), (), s32[]{:S(2)}) async-start(), calls=%async_computation.7 | async-start | bytes 2129920 | tf_op jit(solution)/shard_map/all_gather | solution.py:29
  67.5 479.2 %all-gather.12.cloned.1.call-start = ((), (), s32[]{:S(2)}) async-start(), calls=%async_computation.8 | async-start | bytes 2129920 | tf_op jit(solution)/shard_map/all_gather | solution.py:35
  68.1 525.6 %reduce-scatter.5.cloned.1.call-start = ((), (), s32[]{:S(2)}) async-start(), calls=%async_computation.11 | async-start | bytes 2359296 | tf_op jit(solution)/shard_map/reduce_scatter | solution.py:56
  98.5 2.0 copy-start.4
  103.4 533.9 %reduce-scatter.3.cloned.1.call-start = ((), (), s32[]{:S(2)}) async-start(), calls=%async_computation.9 | async-start | bytes 2359296 | tf_op jit(solution)/shard_map/reduce_scatter | solution.py:38
  132.0 414.7 %copy-start.1 = (bf16[256,4096]{1,0:T(8,128)(2,1)S(1)}, bf16[256,4096]{1,0:T(8,128)(2,1)}, u32[]{:S(2)}) copy-start(bf16[256,4096]{1,0:T(8,128)(2,1)} %all-gather.6.cloned.1.call-done) | copy-start | bytes 6291460
  552.6 0.7 copy-start.2
  552.6 0.7 copy-start.3
  595.7 31.9 %all-to-all-start.2 = ((bf16[64,4,512]{2,1,0:T(4,128)(2,1)}), bf16[64,4,512]{2,1,0:T(4,128)(2,1)S(1)}, u32[]{:S(2)}, u32[]{:S(2)}) async-start(bf16[64,4,512]{2,1,0:T(4,128)(2,1)} %copy.20), calls=%async_computation.4 | async-start | bytes 524288 | tf_op jit(solution)/shard_map/all_to_all | solution.py:62
Sparse Core Ops, SparseCore 0:
  65.6 30.3 all-gather.13
  98.1 33.8 all-gather.5
  135.0 132.0 all-gather.7
  269.9 136.9 all-gather.9
  409.7 136.9 all-gather.11
  549.4 44.2 reduce-scatter.4
  596.6 40.6 reduce-scatter.2
where the time goes:
time: 647 us; the launch traced here: 646 us
  waiting for transfers between devices  537 us (83%)
  blocking collectives  55.4 us (9%)
  matrix products  15.5 us (2%)
  starting transfers between devices  14.6 us (2%)
  between operations  13.6 us (2%)
  local copies, waits for them, and re-layouts  8.1 us (1%)
    all_gather x1, waiting for transfers between devices, shards(): lax.all_gather(shared_down, 'expert', axis=1, tiled=True)  140 us
    all_gather x1, waiting for transfers between devices, shards(): lax.all_gather(shared_up, 'expert', axis=0, tiled=True)  137 us
    all_gather x1, waiting for transfers between devices, shards(): lax.all_gather(shared_gate, 'expert', axis=0, tiled=True)  135 us
    reduce_scatter x1, waiting for transfers between devices, shards(): lax.psum_scatter(e_terms.astype(jnp.bfloat16), 'dp', scatter_dimension=2,...  40.4 us
    all_to_all x1, blocking collectives, shards(): lax.all_to_all(chosen, 'expert', split_axis=1, concat_axis=0, tiled=True)  32.5 us
    all_gather x1, waiting for transfers between devices, shards(): gathered = lax.all_gather(tokens, 'dp', axis=1, tiled=True)  28.6 us
    all_gather x1, waiting for transfers between devices, shards(): arrived = lax.all_gather(slice_part, 'dp', axis=2, tiled=True)  27.9 us
    all_to_all x1, blocking collectives, shards(): lax.all_to_all(outgoing, 'expert', split_axis=0, concat_axis=0, tiled=True)  22.9 us
  transfers between devices with their start and end apart: 8, of which 8 were waited for; matrix products, arithmetic and copies ran while one was open for 3% of the time, Pallas kernels for 0%

commit v1 on v0

v1 whole, which is shorter than its diff:
```python
import functools

import jax
import jax.numpy as jnp
from jax import lax
from jax.experimental import pallas as pl
from jax.experimental.pallas import tpu as pltpu
from jax.sharding import PartitionSpec as P

NC = 2
NY = 4
BF = jnp.bfloat16
F32 = jnp.float32
MESH = pl.DeviceIdType.MESH


def iota(shape, dim):
    return lax.broadcasted_iota(jnp.int32, shape, dim)


def dot(a, b):
    return jnp.dot(a, b, preferred_element_type=F32)


def dot_nt(a, b):
    return lax.dot_general(a, b, (((1,), (1,)), ((), ())), preferred_element_type=F32)


def dot_tn(a, b):
    return lax.dot_general(a, b, (((0,), (0,)), ((), ())), preferred_element_type=F32)


def silu_mul(g, u):
    return (g / (1.0 + jnp.exp(-g)) * u).astype(BF)


def kernel(
    ndp, nex, slots,
    tok, chz, gates, counts, eg, eu, ed, sg, su, sd,
    out,
    wt, tk, pk, c1, c2, onehot, pk0, pk1, pk2, w1, r1, w2, r2, shared_sum,
    et, eq, eun, ev, st, sq, sun, sv,
    ring_s, ring_r, set_s, set_r, x_s, x_r, rs_s, rs_r,
):
    NX = ndp // NC
    NZ = nex // NY
    T, F = tok.shape
    R = nex * slots
    RZ = NY * slots
    RY = NZ * slots
    d = lax.axis_index("dp")
    e = lax.axis_index("expert")
    x, c = d // NC, d % NC
    z, y = e // NY, e % NY
    mate = x * NC + (1 - c)
    WR = sg.shape[0]

    def zmod(v):
        return lax.rem(v + 2 * NZ, NZ)

    def at_z(k):
        return zmod(z + k) * NY + y

    def at_y(k):
        return z * NY + lax.rem(y + k, NY)

    def at_x(k):
        return lax.rem(x + k, NX) * NC + c

    def rc(src, dst, ss, rs, dp=None, ex=None):
        return pltpu.make_async_remote_copy(
            src_ref=src, dst_ref=dst, send_sem=ss, recv_sem=rs,
            device_id=(d if dp is None else dp, e if ex is None else ex), device_id_type=MESH,
        )

    def drain(view, sem):
        pltpu.make_async_copy(view, view, sem).wait()

    bar = pltpu.get_barrier_semaphore()

    def greet(dp, ex):
        pl.semaphore_signal(bar, inc=1, device_id=(dp, ex), device_id_type=MESH)

    def greet_z(k, carry):
        greet(d, at_z(k))
        return carry

    lax.fori_loop(1, NZ, greet_z, 0)
    for k in range(1, NY):
        greet(d, at_y(k))
    for k in range(1, NX):
        greet(at_x(k), e)
    greet(mate, e)

    def wrows(zc, n=1):
        return pl.ds(pl.multiple_of(zc * (NY * WR), NY * WR), NY * WR)

    def wrow1(zc, yc):
        return pl.ds(pl.multiple_of((zc * NY + yc) * WR, WR), WR)

    mine = wrow1(z, y)
    wt[0, mine, :] = sg[...]
    wt[1, mine, :] = su[...]
    wt[2, mine, :] = sd[...]
    tk[d] = tok[...]
    c1[z] = chz[z]
    pl.semaphore_wait(bar, (NZ - 1) + (NY - 1) + (NX - 1) + 1)

    def send_z(i, src, dst):
        def one(k, carry):
            zz = zmod(z + k)
            rc(src(zz), dst, set_s.at[i], set_r.at[i], ex=zz * NY + y).start()
            return carry
        lax.fori_loop(1, NZ, one, 0)

    def send_y(i, src, dst):
        for k in range(1, NY):
            yy = lax.rem(y + k, NY)
            rc(src(yy), dst, set_s.at[i], set_r.at[i], ex=z * NY + yy).start()

    CW = NZ // 2
    CCW = NZ - 1 - CW

    def bsend(k, side):
        rows = wrow1(zmod(z - k) if side == 0 else zmod(z + k), y)
        v = wt.at[pl.ds(0, 2), rows, :]
        return rc(v, v, ring_s.at[0, side, k], ring_r.at[0, side, k], ex=at_z(1 if side == 0 else -1))

    def asend(k, side):
        rows = wrows(zmod(z - k) if side == 0 else zmod(z + k))
        v = wt.at[2, rows, :]
        return rc(v, v, ring_s.at[1, side, k], ring_r.at[1, side, k], ex=at_z(1 if side == 0 else -1))

    def bspread(zc):
        v = wt.at[pl.ds(0, 2), wrow1(zc, y), :]
        send_y(0, lambda yy: v, v)

    def ring_b(k):
        if k == 0:
            bsend(0, 0).start()
            bsend(0, 1).start()
            bspread(z)
            return
        if k <= CW:
            bsend(k - 1, 0).wait_recv()
            if k < CW:
                bsend(k, 0).start()
        if k <= CCW:
            bsend(k - 1, 1).wait_recv()
            if k < CCW:
                bsend(k, 1).start()
        if k <= CW:
            bspread(zmod(z - k))
        if k <= CCW:
            bspread(zmod(z + k))

    def ring_a(k):
        if k == 0:
            asend(0, 0).start()
            asend(0, 1).start()
            return
        if k <= CW:
            asend(k - 1, 0).wait_recv()
            if k < CW:
                asend(k, 0).start()
        if k <= CCW:
            asend(k - 1, 1).wait_recv()
            if k < CCW:
                asend(k, 1).start()

    def dp_own(i, buf):
        for k in range(1, NX):
            rc(buf.at[d], buf.at[d], x_s.at[i, k], x_r.at[i, k], dp=at_x(k)).start()
        rc(buf.at[d], buf.at[d], x_s.at[i, 0], x_r.at[i, 0], dp=mate).start()

    def dp_pass(i, buf):
        order = sorted(range(1, NX), key=lambda k: min(k, NX - k))
        for k in order:
            src = buf.at[at_x(NX - k)]
            rc(src, src, x_s.at[i, k], x_r.at[i, k], dp=at_x(k)).wait_recv()
            rc(src, src, x_s.at[i, 0], x_r.at[i, 0], dp=mate).start()

    def dp_done(i, buf):
        drain(buf.at[pl.ds(0, NX)], x_r.at[i, 0])
        drain(buf.at[pl.ds(0, NX)], x_s.at[i, 0])
        for k in range(1, NX):
            drain(buf.at[0], x_s.at[i, k])

    def rs_start(i, block, tb, qb, ub):
        for n in range(NX):
            xx = lax.rem(x + 1 + n, NX)
            tb[n] = block(xx * NC + (1 - c)).astype(BF)
            rc(tb.at[n], qb.at[n], rs_s.at[i, n], rs_r.at[i, n], dp=mate).start()

    def rs_cross(i, block, tb, qb, ub, vb):
        own = None
        for n in range(NX):
            xx = lax.rem(x + 1 + n, NX)
            val = block(xx * NC + c).astype(BF).astype(F32)
            rc(tb.at[n], qb.at[n], rs_s.at[i, n], rs_r.at[i, n], dp=mate).wait_recv()
            val = val + qb[n].astype(F32)
            if n < NX - 1:
                ub[n] = val.astype(BF)
                rc(ub.at[n], vb.at[n], rs_s.at[i, NX], rs_r.at[i, NX], dp=xx * NC + c).start()
            else:
                own = val
        return own

    def rs_end(i, own, tb, ub, vb):
        drain(vb, rs_r.at[i, NX])
        total = own
        for n in range(NX - 1):
            total = total + vb[n].astype(F32)
        for n in range(NX):
            drain(tb.at[n], rs_s.at[i, n])
        drain(ub, rs_s.at[i, NX])
        return total

    def perm(src):
        r, q = iota((R, R), 0), iota((R, R), 1)
        want = ((r // slots) % NY) * RY + (r // RZ) * slots + r % slots
        return dot((want == q).astype(BF), src).astype(BF)

    def unperm(src):
        r, q = iota((R, R), 0), iota((R, R), 1)
        want = ((r // slots) % NZ) * RZ + (r // RY) * slots + r % slots
        return dot((want == q).astype(BF), src).astype(BF)

    send_z(1, lambda zz: chz.at[zz], c1.at[z])
    dp_own(0, tk)
    vd = wt.at[2, mine, :]
    send_y(2, lambda yy: vd, vd)
    ring_b(0)

    drain(c1.at[pl.ds(0, NZ - 1)], set_r.at[1])
    c2[y] = c1[...]
    send_y(3, lambda yy: c1, c2.at[y])

    drain(wt.at[2, pl.ds(0, (NY - 1) * WR), :], set_r.at[2])
    ring_a(0)
    ring_b(1)

    drain(c2.at[pl.ds(0, NY - 1)], set_r.at[3])
    ids = c2[...].reshape(nex, 128).astype(F32).astype(BF)
    rep = (iota((R, nex), 0) // slots == iota((R, nex), 1)).astype(BF)
    spread = dot(rep, ids)
    lane = y * slots + iota((R, 128), 0) % slots
    pick = jnp.sum(jnp.where(iota((R, 128), 1) == lane, spread, 0.0), axis=1, keepdims=True)
    onehot[...] = (pick.astype(jnp.int32) == iota((R, T), 1)).astype(BF)
    pk0[...] = dot(onehot[...], tok[...]).astype(BF).reshape(NY, RY, F)
    pk1[y] = pk0[y]
    send_y(4, lambda yy: pk0.at[yy], pk1.at[y])

    dp_pass(0, tk)
    ring_b(2)
    ring_a(1)

    drain(pk1.at[pl.ds(0, NY - 1)], set_r.at[4])
    pk2[...] = perm(pk1[...].reshape(R, F)).reshape(NZ, RZ, F)
    pk[d, z] = pk2[z]
    send_z(5, lambda zz: pk2.at[zz], pk.at[d, z])

    ring_b(3)
    ring_a(2)
    ring_b(4)

    drain(pk.at[d, pl.ds(0, NZ - 1)], set_r.at[5])
    dp_own(1, pk)
    ring_a(3)
    ring_b(5)
    dp_pass(1, pk)
    ring_a(4)
    ring_b(6)
    dp_done(1, pk)

    EH = eg.shape[-1]

    def e_step(n, carry):
        a = pk[n].reshape(R, F)
        return carry[0] + dot(a, eg[n]), carry[1] + dot(a, eu[n])

    zero = jnp.zeros((R, EH), F32)
    e_g, e_u = lax.fori_loop(0, ndp, e_step, (zero, zero))
    e_hidden = silu_mul(e_g, e_u)

    def e_block(n):
        return dot(e_hidden, ed[:, pl.ds(pl.multiple_of(n * F, F), F)])

    rs_start(0, e_block, et, eq, eun)
    ring_a(5)
    ring_b(7)
    e_own = rs_cross(0, e_block, et, eq, eun, ev)
    ring_b(8)
    ring_a(6)
    e_sum = rs_end(0, e_own, et, eun, ev)

    live = iota(gates.shape, 0) % slots < counts[...]
    weight = jnp.where(live, gates[...], 0.0)
    reps = R // gates.shape[0]
    tall = jnp.broadcast_to(weight[None], (reps,) + gates.shape).reshape(R, nex)
    column = jnp.sum(
        jnp.where(iota((R, nex), 0) // slots == iota((R, nex), 1), tall, 0.0), axis=1, keepdims=True
    )
    w1[...] = (e_sum * column).astype(BF).reshape(NZ, RZ, F)
    r1[z] = w1[z]
    send_z(6, lambda zz: w1.at[zz], r1.at[z])
    ring_a(7)

    drain(r1.at[pl.ds(0, NZ - 1)], set_r.at[6])
    w2[...] = unperm(r1[...].reshape(R, F)).reshape(NY, RY, F)
    r2[y] = w2[y]
    send_y(7, lambda yy: w2.at[yy], r2.at[y])
    ring_a(8)

    dp_done(0, tk)
    drain(wt.at[pl.ds(0, 2), pl.ds(0, NZ * (NY - 1) * WR), :], set_r.at[0])

    def s_step(n, carry):
        a = tk[n]
        rows = pl.ds(pl.multiple_of(n * F, F), F)
        return carry[0] + dot(a, wt[0, rows, :]), carry[1] + dot(a, wt[1, rows, :])

    zero = jnp.zeros((T, sg.shape[1]), F32)
    s_g, s_u = lax.fori_loop(0, ndp, s_step, (zero, zero))
    s_hidden = silu_mul(s_g, s_u)

    def s_block(n):
        return dot_nt(s_hidden, wt[2, pl.ds(pl.multiple_of(n * F, F), F), :])

    rs_start(1, s_block, st, sq, sun)
    s_own = rs_cross(1, s_block, st, sq, sun, sv)
    drain(r2.at[pl.ds(0, NY - 1)], set_r.at[7])
    routed = dot_tn(onehot[...], r2[...].reshape(R, F))
    shared_sum[...] = s_own + routed
    out[...] = rs_end(1, shared_sum[...], st, sun, sv).astype(BF)

    drain(wt.at[pl.ds(0, 2), pl.ds(0, NZ * (NY - 1) * WR), :], set_s.at[0])
    drain(c1.at[pl.ds(0, NZ - 1)], set_s.at[1])
    drain(wt.at[2, pl.ds(0, (NY - 1) * WR), :], set_s.at[2])
    drain(c2.at[pl.ds(0, NY - 1)], set_s.at[3])
    drain(pk1.at[pl.ds(0, NY - 1)], set_s.at[4])
    drain(pk2.at[pl.ds(0, NZ - 1)], set_s.at[5])
    drain(w1.at[pl.ds(0, NZ - 1)], set_s.at[6])
    drain(r2.at[pl.ds(0, NY - 1)], set_s.at[7])
    for k in range(CW):
        bsend(k, 0).wait_send()
        asend(k, 0).wait_send()
    for k in range(CCW):
        bsend(k, 1).wait_send()
        asend(k, 1).wait_send()


def shards(ndp, nex, tokens, chosen, counts, gates, eg, eu, ed, sg, su, sd):
    NX, NZ = ndp // NC, nex // NY
    slots = chosen.shape[2]
    T, F = tokens.shape
    D = F * ndp
    R = nex * slots
    RZ, RY = NY * slots, NZ * slots
    WR, SHD = sg.shape
    CW = NZ // 2
    chz = jnp.pad(chosen.reshape(NZ, 1, RZ), ((0, 0), (0, 0), (0, 128 - RZ)))
    gt = gates[0].T
    if slots < 8:
        gt = jnp.concatenate([gt] * (8 // slots), axis=0)
    vm = pl.BlockSpec(memory_space=pltpu.VMEM)
    return pl.pallas_call(
        functools.partial(kernel, ndp, nex, slots),
        out_shape=jax.ShapeDtypeStruct((T, F), BF),
        in_specs=[vm] * 10,
        out_specs=vm,
        scratch_shapes=[
            pltpu.VMEM((3, D, SHD), BF),
            pltpu.VMEM((ndp, T, F), BF),
            pltpu.VMEM((ndp, NZ, RZ, F), BF),
            pltpu.VMEM((NZ, 1, 128), jnp.int32),
            pltpu.VMEM((NY, NZ, 1, 128), jnp.int32),
            pltpu.VMEM((R, T), BF),
            pltpu.VMEM((NY, RY, F), BF),
            pltpu.VMEM((NY, RY, F), BF),
            pltpu.VMEM((NZ, RZ, F), BF),
            pltpu.VMEM((NZ, RZ, F), BF),
            pltpu.VMEM((NZ, RZ, F), BF),
            pltpu.VMEM((NY, RY, F), BF),
            pltpu.VMEM((NY, RY, F), BF),
            pltpu.VMEM((T, F), F32),
            pltpu.VMEM((NX, R, F), BF),
            pltpu.VMEM((NX, R, F), BF),
            pltpu.VMEM((NX - 1, R, F), BF),
            pltpu.VMEM((NX - 1, R, F), BF),
            pltpu.VMEM((NX, T, F), BF),
            pltpu.VMEM((NX, T, F), BF),
            pltpu.VMEM((NX - 1, T, F), BF),
            pltpu.VMEM((NX - 1, T, F), BF),
            pltpu.SemaphoreType.DMA((2, 2, CW)),
            pltpu.SemaphoreType.DMA((2, 2, CW)),
            pltpu.SemaphoreType.DMA((8,)),
            pltpu.SemaphoreType.DMA((8,)),
            pltpu.SemaphoreType.DMA((2, NX)),
            pltpu.SemaphoreType.DMA((2, NX)),
            pltpu.SemaphoreType.DMA((2, NX + 1)),
            pltpu.SemaphoreType.DMA((2, NX + 1)),
        ],
        compiler_params=pltpu.CompilerParams(
            collective_id=0, has_side_effects=True, vmem_limit_bytes=48 * 1024 * 1024
        ),
    )(
        tokens, chz, gt, counts,
        eg.reshape(ndp, F, eg.shape[-1]), eu.reshape(ndp, F, eu.shape[-1]), ed[0], sg, su, sd.T,
    )


def solution(mesh):
    return jax.shard_map(
        functools.partial(shards, mesh.shape["dp"], mesh.shape["expert"]),
        mesh=mesh,
        in_specs=(
            P("expert", "dp"),
            P("expert", None, None),
            P("expert", None),
            P("expert", None, None),
            P("expert", None, "dp"),
            P("expert", None, "dp"),
            P("expert", "dp", None),
            P("expert", "dp"),
            P("expert", "dp"),
            P("dp", "expert"),
        ),
        out_specs=P("expert", "dp"),
        check_vma=False,
    )
```

time: 647 us -> 125 us (0.19)
  waiting for transfers between devices: 537 us -> 0 us
  Pallas kernels: 0 us -> 117 us
  blocking collectives: 55.4 us -> 0 us
  matrix products: 15.5 us -> 0 us
  starting transfers between devices: 14.6 us -> 0 us
  between operations: 13.6 us -> 0.04 us
    all_gather x5 -> x0, waiting for transfers between devices: 468 us -> none  [the longest x1 140 us: shards(): lax.all_gather(shared_down, 'expert', axis=1, tiled=True)]
    pallas_call x0 -> x1, Pallas kernels: none -> 117 us  [shards(): pl.pallas_call(functools.partial(kernel, ndp, nex, slots), out_shape=jax....]
    all_to_all x2 -> x0, blocking collectives: 55.4 us -> none  [the longest x1 32.5 us: shards(): lax.all_to_all(chosen, 'expert', split_axis=1, concat_axis=0, tiled=True)]
    reduce_scatter x2 -> x0, waiting for transfers between devices: 50 us -> none  [the longest x1 40.4 us: shards(): lax.psum_scatter(e_terms.astype(jnp.bfloat16), 'dp', scatter_dimension=2,...]
    all_to_all x1 -> x0, waiting for transfers between devices: 16.1 us -> none  [shards(): lax.all_to_all(weighted, 'expert', split_axis=0, concat_axis=0, tiled=True)]
    dot_general x6 -> x0, matrix products: 15.5 us -> none  [the longest x1 5.93 us: shards(): jnp.dot(shared_hidden, lax.all_gather(shared_down, 'expert', axis=1, tile...]
    all_to_all x1 -> x0, starting transfers between devices: 14.3 us -> none  [shards(): lax.all_to_all(weighted, 'expert', split_axis=0, concat_axis=0, tiled=True)]
  transfers between devices with their start and end apart: 8 -> 0, of which waited for: 8 -> 0; matrix products, arithmetic and copies ran while one was open for 3% -> 0% of each run, Pallas kernels for 0% -> 0%
where the time goes in v1:
time: 125 us; the launch traced here: 124 us
  Pallas kernels  117 us (94%)
  local copies, waits for them, and re-layouts  6.87 us (5%)
    pallas_call x1, Pallas kernels, shards(): pl.pallas_call(functools.partial(kernel, ndp, nex, slots), out_shape=jax....  117 us
    unnamed x22, local copies, waits for them, and re-layouts  6.79 us

profile of v1, /device:TPU:1, one launch (start us, length us, event | category | flops | bytes accessed | tf_op | source)
XLA Modules:
  0.0 124.3 jit_solution(7499321054492211008)
XLA Ops:
  0.0 0.0 copy-start.8
  0.0 0.0 copy-start.9
  0.0 0.7 copy-done.8
  0.7 0.0 copy-start.6
  0.7 0.0 copy-done.9
  0.7 0.0 copy-start.5
  0.7 0.1 copy.12
  0.8 0.0 copy-start.4
  0.8 0.1 reshape.9
  0.9 0.0 copy-start.7
  0.9 0.5 copy-done.6
  1.4 0.0 copy-done.5
  1.5 0.1 copy-done.4
  1.6 0.0 copy-done.7
  1.6 0.0 copy-start
  1.6 1.2 copy-done
  2.8 0.0 copy-start.1
  2.8 1.2 copy-done.1
  4.0 0.0 copy-start.2
  4.0 1.2 copy-done.2
  5.3 0.0 copy-start.3
  5.3 0.9 copy-done.3
  6.2 117.3 %shard_map.100 = bf16[256,512]{1,0:T(8,128)(2,1)S(1)} custom-call(bf16[256,512]{1,0:T(8,128)(2,1)S(1)} %copy-done.3, s32[16,1,128]{2,1,0:T(1,128)S(1)} %pad.4.chz, f32[8,64]{1,0:T(8,128)S(1)} %pad_maximum_fusion.gates, s32[1,64]{1,0:T(1,128)S(1)} %copy-done.7, bf16[8,512,128]{2,1,0:T(8,128)(2,1)S(1)} %bitcast.8, bf16[8,512,128]{2,1,0:T(8,128)(2,1)S(1)} %bitcast.9, ...), custom_call_target="tpu_custom_call" | custom-call | tf_op jit(solution)/shard_map/pallas_call | solution.py:367
  123.5 0.7 copy.15
  (2 shorter events, 0.0 us)
Async XLA Ops:
  0.0 0.7 copy-start.8
  0.0 0.7 copy-start.9
  0.7 0.8 copy-start.6
  0.7 0.8 copy-start.5
  0.8 0.8 copy-start.4
  0.9 0.7 copy-start.7
  1.6 1.2 copy-start
  2.8 1.2 copy-start.1
  4.0 1.2 copy-start.2
  5.3 0.9 copy-start.3

commit v2 on v1

v2 whole, which is shorter than its diff:
```python
import functools

import jax
import jax.numpy as jnp
from jax import lax
from jax.experimental import pallas as pl
from jax.experimental.pallas import tpu as pltpu
from jax.sharding import PartitionSpec as P

NC = 2
NY = 4
AH = 1
BF = jnp.bfloat16
F32 = jnp.float32
MESH = pl.DeviceIdType.MESH


def iota(shape, dim):
    return lax.broadcasted_iota(jnp.int32, shape, dim)


def div(v, n):
    return v >> (n.bit_length() - 1)


def mod(v, n):
    return v & (n - 1)


def dot(a, b):
    return jnp.dot(a, b, preferred_element_type=F32)


def dot_nt(a, b):
    return lax.dot_general(a, b, (((1,), (1,)), ((), ())), preferred_element_type=F32)


def dot_tn(a, b):
    return lax.dot_general(a, b, (((0,), (0,)), ((), ())), preferred_element_type=F32)


def silu_mul(g, u):
    return (g / (1.0 + jnp.exp(-g)) * u).astype(BF)


def kernel(
    ndp, nex, slots,
    tok, ch, gates, counts, eg, eu, ed, sg, su, sd,
    out,
    wt, tk, pk, egv, euv, edv, chz, c1, c2, onehot, pm, um, col,
    pk0, pk1, pk2, w1, r1, w2, r2, shared_sum,
    et, eq, eun, ev, st, sq, sun, sv,
    loc, ring_s, ring_r, set_s, set_r, x_s, x_r, rs_s, rs_r,
):
    NX = ndp // NC
    NZ = nex // NY
    T, F = tok.shape
    R = nex * slots
    RZ = NY * slots
    RY = NZ * slots
    HZ = NZ // 2
    RQ = R // 2
    OWN = NZ // 4 - 1
    d = lax.axis_index("dp")
    e = lax.axis_index("expert")
    x, c = div(d, NC), mod(d, NC)
    z, y = div(e, NY), mod(e, NY)
    mate = x * NC + (1 - c)
    WR = sg.shape[0]

    def zmod(v):
        return lax.rem(v + 2 * NZ, NZ)

    def at_z(k):
        return zmod(z + k) * NY + y

    def at_y(k):
        return z * NY + lax.rem(y + k, NY)

    def at_x(k):
        return lax.rem(x + k, NX) * NC + c

    def rc(src, dst, ss, rs, dp=None, ex=None):
        return pltpu.make_async_remote_copy(
            src_ref=src, dst_ref=dst, send_sem=ss, recv_sem=rs,
            device_id=(d if dp is None else dp, e if ex is None else ex), device_id_type=MESH,
        )

    def drain(view, sem):
        pltpu.make_async_copy(view, view, sem).wait()

    bar = pltpu.get_barrier_semaphore()

    def greet(dp, ex):
        pl.semaphore_signal(bar, inc=1, device_id=(dp, ex), device_id_type=MESH)

    def greet_z(k, carry):
        greet(d, at_z(k))
        return carry

    lax.fori_loop(1, NZ, greet_z, 0)
    for k in range(1, NY):
        greet(d, at_y(k))
    for k in range(1, NX):
        greet(at_x(k), e)
    greet(mate, e)

    def wrow1(zc, yc):
        return pl.ds(pl.multiple_of((zc * NY + yc) * WR, WR), WR)

    mine = wrow1(z, y)
    loads = [
        pltpu.make_async_copy(src, dst, loc.at[i])
        for i, (src, dst) in enumerate([
            (sg, wt.at[0, mine, :]), (su, wt.at[1, mine, :]), (sd, wt.at[2, mine, :]), (tok, tk.at[d]),
            (eg, egv), (eu, euv), (ed, edv),
        ])
    ]
    for load in loads:
        load.start()

    ids = jnp.zeros((NZ, 128), F32)
    for s in range(slots):
        row = ch[pl.ds(s, 1), :].astype(F32)
        own = jnp.where(div(iota((NZ, nex), 1), NY) == iota((NZ, nex), 0), row, 0.0).astype(BF)
        place = iota((nex, 128), 1) == mod(iota((nex, 128), 0), NY) * slots + s
        ids = ids + dot(own, place.astype(BF))
    chz[...] = ids.astype(jnp.int32).reshape(NZ, 1, 128)

    r, q = iota((R, R), 0), iota((R, R), 1)
    pm[...] = (mod(div(r, slots), NY) * RY + div(r, RZ) * slots + mod(r, slots) == q).astype(BF)
    zoff = mod(div(r, slots) - z + OWN + NZ, NZ)
    um[...] = (zoff * RZ + div(r, RY) * slots + mod(r, slots) == q).astype(BF)

    live = iota(gates.shape, 0) < counts[...]
    weight = jnp.where(live, gates[...], 0.0)
    for h in range(2):
        r, lane = iota((RQ, nex), 0), iota((RQ, nex), 1)
        owner = mod(z - (h * HZ - OWN) - div(r, RZ) + 2 * NZ, NZ) * NY + mod(div(r, slots), NY)
        picked = jnp.zeros((RQ, nex), F32)
        for s in range(slots):
            picked = jnp.where((lane == owner) & (mod(r, slots) == s), weight[s:s + 1, :], picked)
        col[h] = jnp.sum(picked, axis=1, keepdims=True)

    for load in loads[:4]:
        load.wait()
    pl.semaphore_wait(bar, (NZ - 1) + (NY - 1) + (NX - 1) + 1)

    def send_z(i, src, dst):
        def one(k, carry):
            zz = zmod(z + k)
            rc(src(zz), dst, set_s.at[i], set_r.at[i], ex=zz * NY + y).start()
            return carry
        lax.fori_loop(1, NZ, one, 0)

    def send_slots(i, h, sign, src, dst):
        def one(s, carry):
            zz = zmod(z + sign * (s - OWN))
            rc(src(zz, s - h * HZ), dst(s), set_s.at[i], set_r.at[i], ex=zz * NY + y).start()
            return carry
        if h == 0:
            lax.fori_loop(0, OWN, one, 0)
            lax.fori_loop(OWN + 1, HZ, one, 0)
        else:
            lax.fori_loop(HZ, NZ, one, 0)

    def send_y(i, src, dst):
        for k in range(1, NY):
            yy = lax.rem(y + k, NY)
            rc(src(yy), dst, set_s.at[i], set_r.at[i], ex=z * NY + yy).start()

    CW = NZ // 2
    CCW = NZ - 1 - CW

    def bsend(k, side):
        rows = wrow1(zmod(z - k) if side == 0 else zmod(z + k), y)
        v = wt.at[pl.ds(0, 2), rows, :]
        return rc(v, v, ring_s.at[0, side, k], ring_r.at[0, side, k], ex=at_z(1 if side == 0 else -1))

    def asend(k, side, h):
        zc = zmod(z - k) if side == 0 else zmod(z + k)
        n = NY * WR // AH
        v = wt.at[2, pl.ds(pl.multiple_of(zc * (NY * WR) + h * n, n), n), :]
        return rc(v, v, ring_s.at[1 + h, side, k], ring_r.at[1 + h, side, k], ex=at_z(1 if side == 0 else -1))

    def bspread(zc):
        v = wt.at[pl.ds(0, 2), wrow1(zc, y), :]
        send_y(0, lambda yy: v, v)

    def ring_b(k):
        if k == 0:
            bsend(0, 0).start()
            bsend(0, 1).start()
            bspread(z)
            return
        if k <= CW:
            bsend(k - 1, 0).wait_recv()
            if k < CW:
                bsend(k, 0).start()
        if k <= CCW:
            bsend(k - 1, 1).wait_recv()
            if k < CCW:
                bsend(k, 1).start()
        if k <= CW:
            bspread(zmod(z - k))
        if k <= CCW:
            bspread(zmod(z + k))

    def ring_a(k):
        for h in range(AH):
            if k == 0:
                asend(0, 0, h).start()
                asend(0, 1, h).start()
                continue
            if k <= CW:
                asend(k - 1, 0, h).wait_recv()
                if k < CW:
                    asend(k, 0, h).start()
            if k <= CCW:
                asend(k - 1, 1, h).wait_recv()
                if k < CCW:
                    asend(k, 1, h).start()

    def ring(k):
        if k <= CW:
            ring_b(k)
        if 1 <= k <= CW + 1:
            ring_a(k - 1)

    XORDER = sorted(range(1, NX), key=lambda k: min(k, NX - k))

    def dp_own(i, buf):
        for k in range(1, NX):
            rc(buf(d), buf(d), x_s.at[i, k], x_r.at[i, k], dp=at_x(k)).start()
        rc(buf(d), buf(d), x_s.at[i, 0], x_r.at[i, 0], dp=mate).start()

    def dp_pass(i, buf):
        for k in XORDER:
            src = buf(at_x(NX - k))
            rc(src, src, x_s.at[i, k], x_r.at[i, k], dp=at_x(k)).wait_recv()
            rc(src, src, x_s.at[i, 0], x_r.at[i, 0], dp=mate).start()

    def dp_done(i, buf):
        drain(buf(pl.ds(0, NX)), x_r.at[i, 0])

    def dp_sent(i, buf):
        drain(buf(pl.ds(0, NX)), x_s.at[i, 0])
        for k in range(1, NX):
            drain(buf(0), x_s.at[i, k])

    def rs_start(i, block, tb, qb):
        for n in range(NX):
            xx = lax.rem(x + 1 + n, NX)
            tb[n] = block(xx * NC + (1 - c)).astype(BF)
            rc(tb.at[n], qb.at[n], rs_s.at[i, n], rs_r.at[i, n], dp=mate).start()

    def rs_cross(i, block, tb, qb, ub, vb):
        for n in range(NX):
            xx = lax.rem(x + 1 + n, NX)
            val = block(xx * NC + c).astype(BF).astype(F32)
            rc(tb.at[n], qb.at[n], rs_s.at[i, n], rs_r.at[i, n], dp=mate).wait_recv()
            ub[n] = (val + qb[n].astype(F32)).astype(BF)
            if n < NX - 1:
                rc(ub.at[n], vb.at[n], rs_s.at[i, NX], rs_r.at[i, NX], dp=xx * NC + c).start()

    def rs_end(i, ub, vb):
        drain(vb, rs_r.at[i, NX])
        total = ub[NX - 1].astype(F32)
        for n in range(NX - 1):
            total = total + vb[n].astype(F32)
        return total

    def rs_sent(i, tb, vb):
        for n in range(NX):
            drain(tb.at[n], rs_s.at[i, n])
        drain(vb, rs_s.at[i, NX])

    def tkb(n):
        return tk.at[n]

    def pkb(h):
        return lambda n: pk.at[h, n]

    EH = eg.shape[-1]
    hidden = [None, None, None]

    def e_up(h):
        def step(n, carry):
            a = pk[h, n].reshape(RQ, F)
            return carry[0] + dot(a, egv[n]), carry[1] + dot(a, euv[n])
        zero = jnp.zeros((RQ, EH), F32)
        g, u = lax.fori_loop(0, ndp, step, (zero, zero))
        hidden[h] = silu_mul(g, u)

    def e_block(h):
        return lambda n: dot(hidden[h], edv[:, pl.ds(pl.multiple_of(n * F, F), F)])

    def e_start(h):
        e_up(h)
        rs_start(h, e_block(h), et.at[h], eq.at[h])

    def e_cross(h):
        rs_cross(h, e_block(h), et.at[h], eq.at[h], eun.at[h], ev.at[h])

    def e_end(h):
        w1[h] = (rs_end(h, eun.at[h], ev.at[h]) * col[h]).astype(BF).reshape(HZ, RZ, F)
        if h == 0:
            r1[OWN] = w1[0, OWN]
        send_slots(8 + h, h, -1, lambda zz, s: w1.at[h, s], lambda s: r1.at[s])

    def z_in(h):
        n = HZ - 1 if h == 0 else HZ
        drain(pk.at[h, d, pl.ds(0, n)], set_r.at[5 + h])
        dp_own(1 + h, pkb(h))

    send_z(1, lambda zz: chz.at[zz], c1.at[z])
    vd = wt.at[2, mine, :]
    send_y(2, lambda yy: vd, vd)
    c1[z] = chz[z]
    ring_b(0)
    dp_own(0, tkb)
    drain(wt.at[2, pl.ds(0, (NY - 1) * WR), :], set_r.at[2])
    ring(1)

    drain(c1.at[pl.ds(0, NZ - 1)], set_r.at[1])
    send_y(3, lambda yy: c1, c2.at[y])
    c2[y] = c1[...]
    dp_pass(0, tkb)
    ring(2)

    drain(c2.at[pl.ds(0, NY - 1)], set_r.at[3])
    ids = c2[...].reshape(nex, 128).astype(F32).astype(BF)
    rep = (div(iota((R, nex), 0), slots) == iota((R, nex), 1)).astype(BF)
    spread = dot(rep, ids)
    lane = y * slots + mod(iota((R, 128), 0), slots)
    pick = jnp.sum(jnp.where(iota((R, 128), 1) == lane, spread, 0.0), axis=1, keepdims=True)
    onehot[...] = (pick.astype(jnp.int32) == iota((R, T), 1)).astype(BF)
    pk0[...] = dot(onehot[...], tk[d]).astype(BF).reshape(NY, RY, F)
    send_y(4, lambda yy: pk0.at[yy], pk1.at[y])
    pk1[y] = pk0[y]
    ring(3)

    drain(pk1.at[pl.ds(0, NY - 1)], set_r.at[4])
    pk2[...] = dot(pm[...], pk1[...].reshape(R, F)).astype(BF).reshape(NZ, RZ, F)
    send_slots(5, 0, 1, lambda zz, s: pk2.at[zz], lambda s: pk.at[0, d, s])
    send_slots(6, 1, 1, lambda zz, s: pk2.at[zz], lambda s: pk.at[1, d, s - HZ])
    pk[0, d, OWN] = pk2[z]
    ring(4)

    z_in(0)
    ring(5)
    z_in(1)
    ring(6)
    dp_pass(1, pkb(0))
    for load in loads[4:]:
        load.wait()
    dp_done(1, pkb(0))
    e_start(0)
    e_cross(0)
    ring(7)
    dp_pass(2, pkb(1))
    dp_done(2, pkb(1))
    e_start(1)
    e_cross(1)
    e_end(0)
    ring(8)
    ring(9)

    dp_done(0, tkb)
    drain(wt.at[pl.ds(0, 2), pl.ds(0, NZ * (NY - 1) * WR), :], set_r.at[0])

    def s_step(n, carry):
        a = tk[n]
        rows = pl.ds(pl.multiple_of(n * F, F), F)
        return carry[0] + dot(a, wt[0, rows, :]), carry[1] + dot(a, wt[1, rows, :])

    def s_block(n):
        return dot_nt(s_hidden, wt[2, pl.ds(pl.multiple_of(n * F, F), F), :])

    zero = jnp.zeros((T, sg.shape[1]), F32)
    s_g, s_u = lax.fori_loop(0, ndp, s_step, (zero, zero))
    s_hidden = silu_mul(s_g, s_u)
    rs_start(3, s_block, st, sq)
    e_end(1)
    rs_cross(3, s_block, st, sq, sun, sv)

    drain(r1.at[pl.ds(0, HZ - 1)], set_r.at[8])
    drain(r1.at[pl.ds(0, HZ)], set_r.at[9])
    w2[...] = dot(um[...], r1[...].reshape(R, F)).astype(BF).reshape(NY, RY, F)
    send_y(7, lambda yy: w2.at[yy], r2.at[y])
    r2[y] = w2[y]
    shared_sum[...] = rs_end(3, sun, sv)
    drain(r2.at[pl.ds(0, NY - 1)], set_r.at[7])
    out[...] = (shared_sum[...] + dot_tn(onehot[...], r2[...].reshape(R, F))).astype(BF)

    drain(wt.at[pl.ds(0, 2), pl.ds(0, NZ * (NY - 1) * WR), :], set_s.at[0])
    drain(c1.at[pl.ds(0, NZ - 1)], set_s.at[1])
    drain(wt.at[2, pl.ds(0, (NY - 1) * WR), :], set_s.at[2])
    drain(c2.at[pl.ds(0, NY - 1)], set_s.at[3])
    drain(pk1.at[pl.ds(0, NY - 1)], set_s.at[4])
    drain(pk2.at[pl.ds(0, HZ - 1)], set_s.at[5])
    drain(pk2.at[pl.ds(0, HZ)], set_s.at[6])
    drain(r2.at[pl.ds(0, NY - 1)], set_s.at[7])
    drain(r1.at[pl.ds(0, HZ - 1)], set_s.at[8])
    drain(r1.at[pl.ds(0, HZ)], set_s.at[9])
    dp_sent(0, tkb)
    for h in range(2):
        dp_sent(1 + h, pkb(h))
        rs_sent(h, et.at[h], ev.at[h])
    rs_sent(3, st, sv)
    for side, n in ((0, CW), (1, CCW)):
        for k in range(n):
            bsend(k, side).wait_send()
            for h in range(AH):
                asend(k, side, h).wait_send()


def shards(ndp, nex, tokens, chosen, counts, gates, eg, eu, ed, sg, su, sd):
    NX, NZ = ndp // NC, nex // NY
    slots = chosen.shape[2]
    T, F = tokens.shape
    D = F * ndp
    R = nex * slots
    RZ, RY = NY * slots, NZ * slots
    HZ, RQ = NZ // 2, R // 2
    WR, SHD = sg.shape
    EHD = eg.shape[-1]
    CW = NZ // 2
    vm = pl.BlockSpec(memory_space=pltpu.VMEM)
    hbm = pl.BlockSpec(memory_space=pltpu.HBM)
    return pl.pallas_call(
        functools.partial(kernel, ndp, nex, slots),
        out_shape=jax.ShapeDtypeStruct((T, F), BF),
        in_specs=[hbm, vm, vm, vm] + [hbm] * 6,
        out_specs=vm,
        scratch_shapes=[
            pltpu.VMEM((3, D, SHD), BF),
            pltpu.VMEM((ndp, T, F), BF),
            pltpu.VMEM((2, ndp, HZ, RZ, F), BF),
            pltpu.VMEM((ndp, F, EHD), BF),
            pltpu.VMEM((ndp, F, EHD), BF),
            pltpu.VMEM((EHD, D), BF),
            pltpu.VMEM((NZ, 1, 128), jnp.int32),
            pltpu.VMEM((NZ, 1, 128), jnp.int32),
            pltpu.VMEM((NY, NZ, 1, 128), jnp.int32),
            pltpu.VMEM((R, T), BF),
            pltpu.VMEM((R, R), BF),
            pltpu.VMEM((R, R), BF),
            pltpu.VMEM((2, RQ, 1), F32),
            pltpu.VMEM((NY, RY, F), BF),
            pltpu.VMEM((NY, RY, F), BF),
            pltpu.VMEM((NZ, RZ, F), BF),
            pltpu.VMEM((2, HZ, RZ, F), BF),
            pltpu.VMEM((NZ, RZ, F), BF),
            pltpu.VMEM((NY, RY, F), BF),
            pltpu.VMEM((NY, RY, F), BF),
            pltpu.VMEM((T, F), F32),
            pltpu.VMEM((2, NX, RQ, F), BF),
            pltpu.VMEM((2, NX, RQ, F), BF),
            pltpu.VMEM((2, NX, RQ, F), BF),
            pltpu.VMEM((2, NX - 1, RQ, F), BF),
            pltpu.VMEM((NX, T, F), BF),
            pltpu.VMEM((NX, T, F), BF),
            pltpu.VMEM((NX, T, F), BF),
            pltpu.VMEM((NX - 1, T, F), BF),
            pltpu.SemaphoreType.DMA((7,)),
            pltpu.SemaphoreType.DMA((1 + AH, 2, CW)),
            pltpu.SemaphoreType.DMA((1 + AH, 2, CW)),
            pltpu.SemaphoreType.DMA((10,)),
            pltpu.SemaphoreType.DMA((10,)),
            pltpu.SemaphoreType.DMA((3, NX)),
            pltpu.SemaphoreType.DMA((3, NX)),
            pltpu.SemaphoreType.DMA((4, NX + 1)),
            pltpu.SemaphoreType.DMA((4, NX + 1)),
        ],
        compiler_params=pltpu.CompilerParams(
            collective_id=0, has_side_effects=True, vmem_limit_bytes=60 * 1024 * 1024
        ),
    )(
        tokens, chosen[0].T, gates[0].T, counts,
        eg.reshape(ndp, F, EHD), eu.reshape(ndp, F, EHD), ed[0], sg, su, sd.T,
    )


def solution(mesh):
    return jax.shard_map(
        functools.partial(shards, mesh.shape["dp"], mesh.shape["expert"]),
        mesh=mesh,
        in_specs=(
            P("expert", "dp"),
            P("expert", None, None),
            P("expert", None),
            P("expert", None, None),
            P("expert", None, "dp"),
            P("expert", None, "dp"),
            P("expert", "dp", None),
            P("expert", "dp"),
            P("expert", "dp"),
            P("dp", "expert"),
        ),
        out_specs=P("expert", "dp"),
        check_vma=False,
    )
```

time: 125 us -> 107 us (0.86)
  Pallas kernels: 117 us -> 105 us
  local copies, waits for them, and re-layouts: 6.87 us -> 1.67 us
    pallas_call x1, Pallas kernels: 117 us -> 105 us  [shards(): pl.pallas_call(functools.partial(kernel, ndp, nex, slots), out_shape=jax....]
    unnamed x22 -> x1, local copies, waits for them, and re-layouts: 6.79 us -> 1.67 us
where the time goes in v2:
time: 107 us; the launch traced here: 106 us
  Pallas kernels  105 us (98%)
  local copies, waits for them, and re-layouts  1.67 us (2%)
    pallas_call x1, Pallas kernels, shards(): pl.pallas_call(functools.partial(kernel, ndp, nex, slots), out_shape=jax....  105 us

profile of v2, /device:TPU:1, one launch (start us, length us, event | category | flops | bytes accessed | tf_op | source)
XLA Modules:
  0.0 106.3 jit_solution(8696492804500376888)
XLA Ops:
  0.0 104.6 %shard_map.100 = bf16[256,512]{1,0:T(8,128)(2,1)} custom-call(bf16[256,512]{1,0:T(8,128)(2,1)} %tok.1, s32[4,64]{1,0:T(4,128)} %bitcast.14, f32[4,64]{1,0:T(4,128)} %bitcast.15, s32[1,64]{1,0:T(1,128)} %counts.1, bf16[8,512,128]{2,1,0:T(8,128)(2,1)} %bitcast.10, bf16[8,512,128]{2,1,0:T(8,128)(2,1)} %bitcast.11, bf16[128,4096]{1,0:T(8,128)(2,1)} %bitcast.12, ...), custom_call_target="tpu_custom_call" | custom-call | tf_op jit(solution)/shard_map/pallas_call | solution.py:431
  104.6 1.7 %copy.12 = bf16[256,512]{1,0:T(8,128)(2,1)} copy(bf16[256,512]{1,0:T(8,128)(2,1)} %shard_map.100) | data formatting | bytes 524288

commit v3 on v2

--- a/solution.py
+++ b/solution.py
@@ -9,6 +9,19 @@
 
 NC = 2
 NY = 4
+
+STEPS = (
+    ("start", "dy", "r1", "iz", "r2", "iy", "r3", "oy", "r4", "tk", "z0", "r5", "z1", "r6"),
+    ("g0", "e0", "x0", "r7", "g1", "e1", "x1", "r8", "w0", "r9"),
+    ("su", "w1", "ss", "sx", "bz", "se", "by"),
+)
+
+
+def ORDER(last):
+    names = [name for part in STEPS for name in part]
+    return [n for n in names if not (n[0] == "r" and int(n[1:]) > last)]
+
+
 AH = 1
 BF = jnp.bfloat16
 F32 = jnp.float32
@@ -50,7 +63,7 @@
     wt, tk, pk, egv, euv, edv, chz, c1, c2, onehot, pm, um, col,
     pk0, pk1, pk2, w1, r1, w2, r2, shared_sum,
     et, eq, eun, ev, st, sq, sun, sv,
-    loc, ring_s, ring_r, set_s, set_r, x_s, x_r, rs_s, rs_r,
+    loc, sp_r, ring_s, ring_r, set_s, set_r, x_s, x_r, rs_s, rs_r,
 ):
     NX = ndp // NC
     NZ = nex // NY
@@ -183,15 +196,34 @@
         v = wt.at[2, pl.ds(pl.multiple_of(zc * (NY * WR) + h * n, n), n), :]
         return rc(v, v, ring_s.at[1 + h, side, k], ring_r.at[1 + h, side, k], ex=at_z(1 if side == 0 else -1))
 
-    def bspread(zc):
-        v = wt.at[pl.ds(0, 2), wrow1(zc, y), :]
-        send_y(0, lambda yy: v, v)
+    def spread_to(j, zc, yc, side):
+        v = wt.at[pl.ds(0, 2), wrow1(zc, yc), :]
+        return rc(v, v, set_s.at[0], sp_r.at[side, j], ex=at_y(1 if side == 0 else NY - 1))
+
+    def bspread(j, zc):
+        spread_to(j, zc, y, 0).start()
+        spread_to(j, zc, y, 1).start()
+
+    def bpass(j, zc):
+        for side in range(2):
+            yc = lax.rem(y + (NY - 1 if side == 0 else 1), NY)
+            spread_to(j, zc, yc, side).wait_recv()
+            v = wt.at[side, wrow1(zc, yc), :]
+            rc(v, v, set_s.at[0], set_r.at[0], ex=at_y(1 if side == 0 else NY - 1)).start()
+
+    def bround(k, do):
+        if k == 0:
+            do(0, z)
+        if 1 <= k <= CW:
+            do(2 * k - 1, zmod(z - k))
+        if 1 <= k <= CCW:
+            do(2 * k, zmod(z + k))
 
     def ring_b(k):
         if k == 0:
             bsend(0, 0).start()
             bsend(0, 1).start()
-            bspread(z)
+            bround(0, bspread)
             return
         if k <= CW:
             bsend(k - 1, 0).wait_recv()
@@ -201,10 +233,7 @@
             bsend(k - 1, 1).wait_recv()
             if k < CCW:
                 bsend(k, 1).start()
-        if k <= CW:
-            bspread(zmod(z - k))
-        if k <= CCW:
-            bspread(zmod(z + k))
+        bround(k, bspread)
 
     def ring_a(k):
         for h in range(AH):
@@ -224,6 +253,7 @@
     def ring(k):
         if k <= CW:
             ring_b(k)
+        bround(k - 1, bpass)
         if 1 <= k <= CW + 1:
             ring_a(k - 1)
 
@@ -313,61 +343,47 @@
         drain(pk.at[h, d, pl.ds(0, n)], set_r.at[5 + h])
         dp_own(1 + h, pkb(h))
 
-    send_z(1, lambda zz: chz.at[zz], c1.at[z])
-    vd = wt.at[2, mine, :]
-    send_y(2, lambda yy: vd, vd)
-    c1[z] = chz[z]
-    ring_b(0)
-    dp_own(0, tkb)
-    drain(wt.at[2, pl.ds(0, (NY - 1) * WR), :], set_r.at[2])
-    ring(1)
-
-    drain(c1.at[pl.ds(0, NZ - 1)], set_r.at[1])
-    send_y(3, lambda yy: c1, c2.at[y])
-    c2[y] = c1[...]
-    dp_pass(0, tkb)
-    ring(2)
-
-    drain(c2.at[pl.ds(0, NY - 1)], set_r.at[3])
-    ids = c2[...].reshape(nex, 128).astype(F32).astype(BF)
-    rep = (div(iota((R, nex), 0), slots) == iota((R, nex), 1)).astype(BF)
-    spread = dot(rep, ids)
-    lane = y * slots + mod(iota((R, 128), 0), slots)
-    pick = jnp.sum(jnp.where(iota((R, 128), 1) == lane, spread, 0.0), axis=1, keepdims=True)
-    onehot[...] = (pick.astype(jnp.int32) == iota((R, T), 1)).astype(BF)
-    pk0[...] = dot(onehot[...], tk[d]).astype(BF).reshape(NY, RY, F)
-    send_y(4, lambda yy: pk0.at[yy], pk1.at[y])
-    pk1[y] = pk0[y]
-    ring(3)
-
-    drain(pk1.at[pl.ds(0, NY - 1)], set_r.at[4])
-    pk2[...] = dot(pm[...], pk1[...].reshape(R, F)).astype(BF).reshape(NZ, RZ, F)
-    send_slots(5, 0, 1, lambda zz, s: pk2.at[zz], lambda s: pk.at[0, d, s])
-    send_slots(6, 1, 1, lambda zz, s: pk2.at[zz], lambda s: pk.at[1, d, s - HZ])
-    pk[0, d, OWN] = pk2[z]
-    ring(4)
-
-    z_in(0)
-    ring(5)
-    z_in(1)
-    ring(6)
-    dp_pass(1, pkb(0))
-    for load in loads[4:]:
-        load.wait()
-    dp_done(1, pkb(0))
-    e_start(0)
-    e_cross(0)
-    ring(7)
-    dp_pass(2, pkb(1))
-    dp_done(2, pkb(1))
-    e_start(1)
-    e_cross(1)
-    e_end(0)
-    ring(8)
-    ring(9)
-
-    dp_done(0, tkb)
-    drain(wt.at[pl.ds(0, 2), pl.ds(0, NZ * (NY - 1) * WR), :], set_r.at[0])
+    def start():
+        send_z(1, lambda zz: chz.at[zz], c1.at[z])
+        vd = wt.at[2, mine, :]
+        send_y(2, lambda yy: vd, vd)
+        c1[z] = chz[z]
+        ring_b(0)
+        dp_own(0, tkb)
+
+    def down_y():
+        drain(wt.at[2, pl.ds(0, (NY - 1) * WR), :], set_r.at[2])
+
+    def ids_z():
+        drain(c1.at[pl.ds(0, NZ - 1)], set_r.at[1])
+        send_y(3, lambda yy: c1, c2.at[y])
+        c2[y] = c1[...]
+
+    def ids_y():
+        drain(c2.at[pl.ds(0, NY - 1)], set_r.at[3])
+        ids = c2[...].reshape(nex, 128).astype(F32).astype(BF)
+        rep = (div(iota((R, nex), 0), slots) == iota((R, nex), 1)).astype(BF)
+        spread = dot(rep, ids)
+        lane = y * slots + mod(iota((R, 128), 0), slots)
+        pick = jnp.sum(jnp.where(iota((R, 128), 1) == lane, spread, 0.0), axis=1, keepdims=True)
+        onehot[...] = (pick.astype(jnp.int32) == iota((R, T), 1)).astype(BF)
+        pk0[...] = dot(onehot[...], tk[d]).astype(BF).reshape(NY, RY, F)
+        send_y(4, lambda yy: pk0.at[yy], pk1.at[y])
+        pk1[y] = pk0[y]
+
+    def out_y():
+        drain(pk1.at[pl.ds(0, NY - 1)], set_r.at[4])
+        pk2[...] = dot(pm[...], pk1[...].reshape(R, F)).astype(BF).reshape(NZ, RZ, F)
+        send_slots(5, 0, 1, lambda zz, s: pk2.at[zz], lambda s: pk.at[0, d, s])
+        send_slots(6, 1, 1, lambda zz, s: pk2.at[zz], lambda s: pk.at[1, d, s - HZ])
+        pk[0, d, OWN] = pk2[z]
+
+    def gathered(h):
+        dp_pass(1 + h, pkb(h))
+        if h == 0:
+            for load in loads[4:]:
+                load.wait()
+        dp_done(1 + h, pkb(h))
 
     def s_step(n, carry):
         a = tk[n]
@@ -375,23 +391,40 @@
         return carry[0] + dot(a, wt[0, rows, :]), carry[1] + dot(a, wt[1, rows, :])
 
     def s_block(n):
-        return dot_nt(s_hidden, wt[2, pl.ds(pl.multiple_of(n * F, F), F), :])
-
-    zero = jnp.zeros((T, sg.shape[1]), F32)
-    s_g, s_u = lax.fori_loop(0, ndp, s_step, (zero, zero))
-    s_hidden = silu_mul(s_g, s_u)
-    rs_start(3, s_block, st, sq)
-    e_end(1)
-    rs_cross(3, s_block, st, sq, sun, sv)
-
-    drain(r1.at[pl.ds(0, HZ - 1)], set_r.at[8])
-    drain(r1.at[pl.ds(0, HZ)], set_r.at[9])
-    w2[...] = dot(um[...], r1[...].reshape(R, F)).astype(BF).reshape(NY, RY, F)
-    send_y(7, lambda yy: w2.at[yy], r2.at[y])
-    r2[y] = w2[y]
-    shared_sum[...] = rs_end(3, sun, sv)
-    drain(r2.at[pl.ds(0, NY - 1)], set_r.at[7])
-    out[...] = (shared_sum[...] + dot_tn(onehot[...], r2[...].reshape(R, F))).astype(BF)
+        return dot_nt(hidden[2], wt[2, pl.ds(pl.multiple_of(n * F, F), F), :])
+
+    def s_up():
+        dp_done(0, tkb)
+        drain(wt.at[pl.ds(0, 2), pl.ds(0, NZ * WR), :], set_r.at[0])
+        zero = jnp.zeros((T, sg.shape[1]), F32)
+        g, u = lax.fori_loop(0, ndp, s_step, (zero, zero))
+        hidden[2] = silu_mul(g, u)
+
+    def back_z():
+        drain(r1.at[pl.ds(0, HZ - 1)], set_r.at[8])
+        drain(r1.at[pl.ds(0, HZ)], set_r.at[9])
+        w2[...] = dot(um[...], r1[...].reshape(R, F)).astype(BF).reshape(NY, RY, F)
+        send_y(7, lambda yy: w2.at[yy], r2.at[y])
+        r2[y] = w2[y]
+
+    def s_end():
+        shared_sum[...] = rs_end(3, sun, sv)
+
+    def back_y():
+        drain(r2.at[pl.ds(0, NY - 1)], set_r.at[7])
+        out[...] = (shared_sum[...] + dot_tn(onehot[...], r2[...].reshape(R, F))).astype(BF)
+
+    steps = {
+        "start": start, "dy": down_y, "iz": ids_z, "iy": ids_y, "oy": out_y, "tk": lambda: dp_pass(0, tkb),
+        "z0": lambda: z_in(0), "z1": lambda: z_in(1), "g0": lambda: gathered(0), "g1": lambda: gathered(1),
+        "e0": lambda: e_start(0), "e1": lambda: e_start(1), "x0": lambda: e_cross(0), "x1": lambda: e_cross(1),
+        "w0": lambda: e_end(0), "w1": lambda: e_end(1), "su": s_up, "ss": lambda: rs_start(3, s_block, st, sq),
+        "sx": lambda: rs_cross(3, s_block, st, sq, sun, sv), "bz": back_z, "se": s_end, "by": back_y,
+    }
+    for k in range(1, CW + 2):
+        steps[f"r{k}"] = functools.partial(ring, k)
+    for name in ORDER(CW + 1):
+        steps[name]()
 
     drain(wt.at[pl.ds(0, 2), pl.ds(0, NZ * (NY - 1) * WR), :], set_s.at[0])
     drain(c1.at[pl.ds(0, NZ - 1)], set_s.at[1])
@@ -464,6 +497,7 @@
             pltpu.VMEM((NX, T, F), BF),
             pltpu.VMEM((NX - 1, T, F), BF),
             pltpu.SemaphoreType.DMA((7,)),
+            pltpu.SemaphoreType.DMA((2, NZ)),
             pltpu.SemaphoreType.DMA((1 + AH, 2, CW)),
             pltpu.SemaphoreType.DMA((1 + AH, 2, CW)),
             pltpu.SemaphoreType.DMA((10,)),

time: 107 us -> 101 us (0.944)
  Pallas kernels: 105 us -> 99.1 us
    pallas_call x1, Pallas kernels: 105 us -> 99.1 us  [shards(): pl.pallas_call(functools.partial(kernel, ndp, nex, slots), out_shape=jax....]
where the time goes in v3:
time: 101 us
  Pallas kernels  99.1 us (98%)
  local copies, waits for them, and re-layouts  1.67 us (2%)
    pallas_call x1, Pallas kernels, shards(): pl.pallas_call(functools.partial(kernel, ndp, nex, slots), out_shape=jax....  99.1 us

profile of v3, /device:TPU:1, one launch (start us, length us, event | category | flops | bytes accessed | tf_op | source)
XLA Modules:
  0.0 100.8 jit_solution(14523925259845926844)
XLA Ops:
  0.0 99.1 %shard_map.100 = bf16[256,512]{1,0:T(8,128)(2,1)} custom-call(bf16[256,512]{1,0:T(8,128)(2,1)} %tok.1, s32[4,64]{1,0:T(4,128)} %bitcast.14, f32[4,64]{1,0:T(4,128)} %bitcast.15, s32[1,64]{1,0:T(1,128)} %counts.1, bf16[8,512,128]{2,1,0:T(8,128)(2,1)} %bitcast.10, bf16[8,512,128]{2,1,0:T(8,128)(2,1)} %bitcast.11, bf16[128,4096]{1,0:T(8,128)(2,1)} %bitcast.12, ...), custom_call_target="tpu_custom_call" | custom-call | tf_op jit(solution)/shard_map/pallas_call | solution.py:464
  99.1 1.7 %copy.12 = bf16[256,512]{1,0:T(8,128)(2,1)} copy(bf16[256,512]{1,0:T(8,128)(2,1)} %shard_map.100) | data formatting | bytes 524288

commit v4 on v3

--- a/solution.py
+++ b/solution.py
@@ -12,7 +12,7 @@
 
 STEPS = (
     ("start", "dy", "r1", "iz", "r2", "iy", "r3", "oy", "r4", "tk", "z0", "r5", "z1", "r6"),
-    ("g0", "e0", "x0", "r7", "g1", "e1", "x1", "r8", "w0", "r9"),
+    ("g0", "e0", "x0", "r7", "g1", "e1", "x1", "r8", "r9", "w0"),
     ("su", "w1", "ss", "sx", "bz", "se", "by"),
 )
 

time: 101 us -> 100 us (0.990)
  no operation moved by 1% of the time
where the time goes in v4:
time: 100 us; the launch traced here: 99.9 us
  Pallas kernels  98.2 us (98%)
  local copies, waits for them, and re-layouts  1.67 us (2%)
    pallas_call x1, Pallas kernels, shards(): pl.pallas_call(functools.partial(kernel, ndp, nex, slots), out_shape=jax....  98.2 us

profile of v4, /device:TPU:1, one launch (start us, length us, event | category | flops | bytes accessed | tf_op | source)
XLA Modules:
  0.0 99.9 jit_solution(10218148177955336841)
XLA Ops:
  0.0 98.2 %shard_map.100 = bf16[256,512]{1,0:T(8,128)(2,1)} custom-call(bf16[256,512]{1,0:T(8,128)(2,1)} %tok.1, s32[4,64]{1,0:T(4,128)} %bitcast.14, f32[4,64]{1,0:T(4,128)} %bitcast.15, s32[1,64]{1,0:T(1,128)} %counts.1, bf16[8,512,128]{2,1,0:T(8,128)(2,1)} %bitcast.10, bf16[8,512,128]{2,1,0:T(8,128)(2,1)} %bitcast.11, bf16[128,4096]{1,0:T(8,128)(2,1)} %bitcast.12, ...), custom_call_target="tpu_custom_call" | custom-call | tf_op jit(solution)/shard_map/pallas_call | solution.py:464
  98.2 1.7 %copy.12 = bf16[256,512]{1,0:T(8,128)(2,1)} copy(bf16[256,512]{1,0:T(8,128)(2,1)} %shard_map.100) | data formatting | bytes 524288
